TPU v7x, 32 devices: a whole 2x2x4 slice. The times are simulated.
32 devices in a mesh: seq: 8 (over z, y), head: 4 (over x, core).
Axes of the slice: x: 2, y: 2, z: 4, core: 2. Of those that a mesh axis runs over, the one named last changes fastest.
Arguments:
- queries: bfloat16 [4096, 32, 128], P('seq', 'head'), may hold values from -6 to 6
- key_matrix: bfloat16 [4096, 32, 128], P('seq', 'head'), may hold values from -6 to 6
- value_matrix: bfloat16 [4096, 32, 128], P('seq', 'head'), may hold values from -6 to 6
- level_weight: float32 [13, 32, 4096], P(None, 'head', 'seq'), may hold values from 0.25 to 4
- out_weight: bfloat16 [32, 128, 4096], P('head'), may hold values from -0.09375 to 0.09375
- grad_out: bfloat16 [4096, 4096], P('seq', 'head'), may hold values from -4 to 4
Outputs:
- mixed_out: bfloat16 [4096, 4096], P('seq', 'head')
- grad_queries: bfloat16 [4096, 32, 128], P('seq', 'head')
- grad_keys: bfloat16 [4096, 32, 128], P('seq', 'head')
- grad_values: bfloat16 [4096, 32, 128], P('seq', 'head')
- grad_levels: float32 [13, 32, 4096], P(None, 'head', 'seq')
All inputs are finite; a program needn't handle non-finite values.
Results may differ from a plain program's by a relative error of at most 0.017.
Values may be sent and summed in bfloat16 or wider, within the bound.
A program may use at most 128 MiB of HBM per device.

v0:
```python
import jax
import jax.numpy as jnp
from jax import lax
from jax.sharding import PartitionSpec as P

PRECISE_MATCH = lax.Precision.HIGHEST


def partner_2(block, axis, distance):
    count = lax.axis_size(axis)
    route = []
    for low in range(count):
        high = low | 1 << distance
        if high != low and high < count:
            route += [(low, high), (high, low)]
    return lax.ppermute(block, axis, route)


def top_bit(differ, bit_total):
    count_bits = jnp.zeros(differ.shape, jnp.int32)
    for exponent in range(bit_total):
        count_bits = count_bits + (differ >= 2**exponent).astype(jnp.int32)
    return count_bits


def level_scales(level_total, head_width):
    raised = jnp.maximum(jnp.arange(level_total, dtype=jnp.int32) - 1, 0).astype(jnp.float32)
    return jnp.exp2(-0.5 * raised) / jnp.sqrt(jnp.float32(head_width))


def two_parts(exact_state):
    upper = exact_state.astype(jnp.bfloat16)
    lower = (exact_state - upper.astype(jnp.float32)).astype(jnp.bfloat16)
    return (upper, lower)


def state_first(form, exact_state, plain):
    upper, lower = two_parts(exact_state)
    return jnp.einsum(form, upper, plain, preferred_element_type=jnp.float32) + jnp.einsum(
        form, lower, plain, preferred_element_type=jnp.float32
    )


def state_second(form, plain, exact_state):
    upper, lower = two_parts(exact_state)
    return jnp.einsum(form, plain, upper, preferred_element_type=jnp.float32) + jnp.einsum(
        form, plain, lower, preferred_element_type=jnp.float32
    )


def on_device(queries, key_matrix, value_matrix, level_weight, out_weight, grad_out):
    rows_dev, head_count, head_width = queries.shape
    level_total = level_weight.shape[0]
    near_levels = rows_dev.bit_length()
    far_levels = lax.axis_size("seq").bit_length() - 1
    my_block = lax.axis_index("seq")
    scales = level_scales(level_total, head_width)
    weighted_levels = level_weight * scales[:, None, None]
    flat_out = out_weight.reshape(head_count * head_width, out_weight.shape[2])
    columns = flat_out
    mix_sum = lax.dot_general(
        lax.all_gather(grad_out, "head", axis=1, tiled=True),
        columns,
        (((1,), (1,)), ((), ())),
        preferred_element_type=jnp.float32,
    )
    grad_mix = mix_sum.astype(jnp.bfloat16).reshape(rows_dev, head_count, head_width)
    mix_f = grad_mix.astype(jnp.float32)
    key_weighted = jnp.einsum(
        "gpl,gpq->plq", key_matrix, value_matrix, preferred_element_type=jnp.float32
    )
    far_weights = weighted_levels[near_levels:]
    weighted = (
        far_weights[:, :, :, None] * jnp.transpose(queries.astype(jnp.float32), (1, 0, 2))[None]
    )
    back_states = state_first("jhik,ihv->jhkv", weighted, grad_mix)
    every = lax.all_gather(
        key_weighted[None].astype(jnp.bfloat16), "seq", axis=0, tiled=True
    ).astype(jnp.float32)
    block_ids = jnp.arange(every.shape[0], dtype=jnp.int32)
    block_gap = top_bit(jnp.bitwise_xor(block_ids, my_block), far_levels)
    level_ladder = jnp.arange(1, far_levels + 1, dtype=jnp.int32)
    masks = ((block_gap[None] == level_ladder[:, None]) & (block_ids < my_block)[None]).astype(
        jnp.float32
    )
    left_states = jnp.einsum("je,ehkv->jhkv", masks, every, precision=PRECISE_MATCH)
    pending = back_states
    right_list = []
    for bit_index in range(far_levels):
        partner = partner_2(pending.astype(jnp.bfloat16), "seq", bit_index).astype(pending.dtype)
        bit_off = 1.0 - (my_block // 2**bit_index % 2).astype(jnp.float32)
        right_list.append(bit_off * partner[0])
        pending = pending[1:] + partner[1:]
    right_states = jnp.stack(right_list)
    rows_index = lax.broadcasted_iota(jnp.int32, (rows_dev, near_levels, rows_dev), 0)
    tier_index = lax.broadcasted_iota(jnp.int32, (rows_dev, near_levels, rows_dev), 1)
    cols_index = lax.broadcasted_iota(jnp.int32, (rows_dev, near_levels, rows_dev), 2)
    near_gap = top_bit(jnp.bitwise_xor(rows_index, cols_index), near_levels - 1)
    onehot = ((near_gap == tier_index) & (cols_index <= rows_index)).astype(jnp.float32)
    mixing = jnp.einsum(
        "ilj,lhi->hij", onehot, weighted_levels[:near_levels], precision=PRECISE_MATCH
    )
    scores = jnp.einsum("ihk,jhk->hij", queries, key_matrix, preferred_element_type=jnp.float32)
    attention = (scores * mixing).astype(jnp.bfloat16)
    local_out = jnp.einsum(
        "hij,jhv->ihv", attention, value_matrix, preferred_element_type=jnp.float32
    )
    far_rows = jnp.transpose(far_weights, (0, 2, 1))[..., None]
    reads = state_second("ihk,jhkv->jihv", queries, left_states)
    attended = (local_out + jnp.sum(far_rows * reads, axis=0)).astype(jnp.bfloat16)
    flat_att = attended.reshape(rows_dev, head_count * head_width)
    columns = flat_out
    mixed_cols = lax.psum_scatter(
        lax.dot_general(
            columns, flat_att, (((0,), (1,)), ((), ())), preferred_element_type=jnp.float32
        ).astype(jnp.bfloat16),
        "head",
        scatter_dimension=0,
        tiled=True,
    ).astype(jnp.float32)
    mixed_out = jnp.transpose(mixed_cols).astype(jnp.bfloat16)
    back = jnp.einsum("ihv,jhv->hij", grad_mix, value_matrix, preferred_element_type=jnp.float32)
    near_grad = (
        jnp.einsum("ilj,hij->lhi", onehot, scores * back, precision=PRECISE_MATCH)
        * scales[:near_levels, None, None]
    )
    far_grad = (
        jnp.transpose(jnp.sum(reads * mix_f[None], axis=3), (0, 2, 1))
        * scales[near_levels:, None, None]
    )
    grad_score = (back * mixing).astype(jnp.bfloat16)
    grad_queries = jnp.einsum(
        "hij,jhk->ihk", grad_score, key_matrix, preferred_element_type=jnp.float32
    )
    grad_queries = grad_queries + jnp.sum(
        far_rows * state_first("jhkv,ihv->jihk", left_states, grad_mix), axis=0
    )
    grad_keys = jnp.einsum("hij,ihk->jhk", grad_score, queries, preferred_element_type=jnp.float32)
    grad_keys = grad_keys + state_first("jhkv,ihv->ihk", right_states, value_matrix)
    grad_values = jnp.einsum(
        "hij,ihv->jhv", attention, grad_mix, preferred_element_type=jnp.float32
    )
    grad_values = grad_values + state_first("jhkv,ihk->ihv", right_states, key_matrix)
    grad_levels = jnp.concatenate([near_grad, far_grad], 0)
    return (
        mixed_out,
        grad_queries.astype(jnp.bfloat16),
        grad_keys.astype(jnp.bfloat16),
        grad_values.astype(jnp.bfloat16),
        grad_levels,
    )


def solution(mesh):
    in_specs = (
        P("seq", "head", None),
        P("seq", "head", None),
        P("seq", "head", None),
        P(None, "head", "seq"),
        P("head", None, None),
        P("seq", "head"),
    )
    out_specs = (
        P("seq", "head"),
        P("seq", "head", None),
        P("seq", "head", None),
        P("seq", "head", None),
        P(None, "head", "seq"),
    )
    return jax.shard_map(
        on_device, mesh=mesh, in_specs=in_specs, out_specs=out_specs, check_vma=False
    )
```

profile of v0, /device:TPU:0, one launch (start us, length us, event | category | flops | bytes accessed | tf_op | source)
XLA Modules:
  0.0 245.9 jit_solution(17869283981879571460)
XLA Ops:
  7.2 1.2 copy-done
  8.4 2.5 %convolution_convert_fusion.1 = bf16[8,128,128]{2,1,0:T(8,128)(2,1)} fusion(bf16[512,8,128]{2,1,0:T(8,128)(2,1)S(1)} %copy-done, bf16[512,8,128]{2,1,0:T(8,128)(2,1)} %param.7), kind=kOutput, calls=%fused_computation.60 | convolution fusion | flops 134348800 | bytes 2359296 | tf_op jit(solution)/shard_map/gpl,gpq->plq/dot_general | solution.py:69
  12.9 1.3 copy-done.13
  14.2 2.6 %fusion.100 = (f32[3,8,512]{0,1,2:T(8,128)}, f32[3,512,8]{0,2,1:T(8,128)}) fusion(f32[13,8,512]{0,1,2:T(8,128)S(1)} %broadcast_multiply_fusion), kind=kLoop, calls=%fused_computation.131 | loop fusion | bytes 147456 | tf_op jit(solution)/shard_map/slice | solution.py:72
  16.8 2.2 copy.171
  19.2 1.8 copy.172
  20.9 2.3 copy.148
  23.2 18.0 %fusion.15 = f32[512,8,512]{2,1,0:T(8,128)} fusion(f32[13,8,512]{0,1,2:T(8,128)} %copy-done.13), kind=kOutput, calls=%fused_computation.22 | convolution fusion | flops 330301440 | bytes 8601600 | tf_op jit(solution)/shard_map/ilj,lhi->hij/dot_general | solution.py:100
  41.2 21.9 %all-gather.6.cloned.1.call-done = bf16[64,128,128]{2,1,0:T(8,128)(2,1)} async-done(((bf16[8,128,128]{2,1,0:T(8,128)(2,1)}), bf16[64,128,128]{2,1,0:T(8,128)(2,1)}) %all-gather.6.cloned.1.call-update) | async-done | bytes 2097168 | tf_op jit(solution)/shard_map/all_gather | solution.py:77
  63.1 3.0 %fusion.33 = f32[3,8,128,128]{3,0,2,1:T(4,128)S(1)} fusion(bf16[8,8,128,128]{3,2,1,0:T(8,128)(2,1)} %bitcast.92, s32[8]{0:T(128)S(1)} %fusion.79, pred[8]{0:T(512)(128)(4,1)S(1)} %iota_compare_fusion.2, s32[3]{0:T(128)S(1)} %iota_add_fusion), kind=kOutput, calls=%fused_computation.44 | convolution fusion | flops 6291504 | bytes 3670068 | tf_op jit(solution)/shard_map/je,ehkv->jhkv/dot_general | solution.py:86
  66.2 1.3 copy-done.3
  67.5 3.8 %fusion.44 = f32[8,3,128,512]{3,2,1,0:T(8,128)} fusion(bf16[512,8,128,1]{2,1,0,3:T(8,128)(2,1)S(1)} %bitcast.88, f32[3,8,128,128]{3,0,2,1:T(4,128)S(1)} %fusion.33), kind=kOutput, calls=%fused_computation.63 | convolution fusion | flops 404226048 | bytes 8912896 | tf_op jit(solution)/shard_map/ihk,jhkv->jihv/dot_general | solution.py:46
  71.3 26.4 %all-gather.4.cloned.1.call-done = bf16[512,4096]{1,0:T(8,128)(2,1)} async-done(((bf16[512,1024]{1,0:T(8,128)(2,1)}), bf16[512,4096]{1,0:T(8,128)(2,1)}) %all-gather.4.cloned.1.call-update) | async-done | bytes 4194320 | tf_op jit(solution)/shard_map/all_gather | solution.py:62
  97.7 9.2 %fusion.42 = bf16[64,8,8,128]{3,1,2,0:T(8,128)(2,1)S(1)} fusion(bf16[512,4096]{1,0:T(8,128)(2,1)} %all-gather.4.cloned.1.call-done, bf16[1024,4096]{1,0:T(8,128)(2,1)} %bitcast.94), kind=kOutput, calls=%fused_computation.57 | convolution fusion | flops 4295491584 | bytes 13631488 | tf_op jit(solution)/shard_map/dot_general | solution.py:61
  106.9 1.2 copy.221
  108.1 1.8 copy.181
  110.0 4.5 %fusion.60 = f32[8,512,512]{2,1,0:T(8,128)} fusion(bf16[512,8,128]{0,2,1:T(8,128)(2,1)S(1)} %copy.181, bf16[512,8,128]{2,1,0:T(8,128)(2,1)S(1)} %copy-done), kind=kOutput, calls=%fused_computation.79 | convolution fusion | flops 536870912 | bytes 10485760 | tf_op jit(solution)/shard_map/ihv,jhv->hij/dot_general | solution.py:122
  114.5 1.6 convert_element_type.240
  116.1 1.6 copy.201
  117.8 7.3 %fusion.20 = (f32[3,512,8]{1,0,2:T(4,128)S(1)}, f32[512,8,128]{0,2,1:T(8,128)}) fusion(f32[512,8,128]{0,2,1:T(8,128)} %convert_element_type.240, f32[8,3,128,512]{3,2,1,0:T(8,128)} %fusion.44, f32[3,512,8]{1,0,2:T(4,128)S(1)} %copy.148, bf16[512,8,128,1]{2,1,0,3:T(8,128)(2,1)S(1)} %bitcast.89, f32[3,8,128,128]{3,0,2,1:T(4,128)} %copy-done.3), kind=kOutput, calls=%fused_computation.29 | convolution fusion | flops 409980928 | bytes 13205504 | tf_op jit(solution)/shard_map/ihk,jhkv->jihv/dot_general | solution.py:46
  125.1 2.9 %copy.158 = f32[512,8,128]{2,0,1:T(8,128)} copy(f32[512,8,128]{0,2,1:T(8,128)} %get-tuple-element.26) | data formatting | bytes 4194304 | tf_op jit(solution)/shard_map/reduce_sum | solution.py:110
  128.0 13.8 %fusion.99 = (f32[8,512,512]{2,1,0:T(8,128)}, bf16[8,512,512]{2,1,0:T(8,128)(2,1)}, bf16[8,512,512]{2,1,0:T(8,128)(2,1)}) fusion(f32[8,512,512]{2,1,0:T(8,128)} %fusion.60, f32[512,8,512]{2,1,0:T(8,128)} %fusion.15, bf16[512,8,128]{2,1,0:T(8,128)(2,1)} %param.7, bf16[512,8,128]{2,1,0:T(8,128)(2,1)S(1)} %copy-done.2), kind=kOutput, calls=%fused_computation.130 | convolution fusion | flops 547356672 | bytes 35651584 | tf_op jit(solution)/shard_map/ihk,jhk->hij/dot_general | solution.py:103
  141.8 12.4 %fusion.21 = bf16[4096,512]{0,1:T(8,128)(2,1)} fusion(bf16[8,128,4096]{2,1,0:T(8,128)(2,1)} %param.10, f32[512,8,128]{2,0,1:T(8,128)} %copy.158, bf16[8,512,512]{2,1,0:T(8,128)(2,1)} %get-tuple-element.33, bf16[512,8,128]{2,1,0:T(8,128)(2,1)S(1)} %copy-done), kind=kOutput, calls=%fused_computation.30 | convolution fusion | flops 4834983936 | bytes 19922944 | tf_op jit(solution)/shard_map/dot_general | solution.py:114
  154.2 6.4 %fusion.22 = f32[8,128,3,128]{3,1,2,0:T(8,128)S(1)} fusion(bf16[512,8,128,1]{0,2,3,1:T(8,128)(2,1)S(1)} %copy.201, f32[8,512,128]{2,1,0:T(8,128)} %copy.172, f32[3,8,512]{2,0,1:T(4,128)S(1)} %copy.171), kind=kOutput, calls=%fused_computation.31 | convolution fusion | flops 405798912 | bytes 4767744 | tf_op jit(solution)/shard_map/jhik,ihv->jhkv/dot_general | solution.py:39
  160.6 3.5 %fusion.101 = (bf16[3,8,128,128]{2,3,0,1:T(8,128)(2,1)}, f32[3,8,128,128]{2,3,0,1:T(8,128)S(1)}) fusion(f32[8,128,3,128]{3,1,2,0:T(8,128)S(1)} %fusion.22, bf16[512,8,128,1]{0,2,3,1:T(8,128)(2,1)S(1)} %copy.201, f32[8,512,128]{2,1,0:T(8,128)S(1)} %copy-done.5, f32[3,8,512]{2,0,1:T(4,128)S(1)} %copy.171), kind=kOutput, calls=%fused_computation.132 | convolution fusion | flops 411303936 | bytes 7127040 | tf_op jit(solution)/shard_map/jhik,ihv->jhkv/dot_general | solution.py:39
  164.2 1.5 collective-permute-start
  165.7 2.1 fusion.102
  168.7 1.1 copy-done.10
  169.9 22.0 %multiply_bitcast_fusion = f32[10,8,512]{0,1,2:T(8,128)} fusion(f32[8,512,512]{2,1,0:T(8,128)S(1)} %copy-done.10, f32[10]{0:T(128)S(1)} %bitcast.93), kind=kOutput, calls=%fused_computation.47 | convolution fusion | flops 330342400 | bytes 8552488 | tf_op jit(solution)/shard_map/ilj,hij->lhi/dot_general | solution.py:124
  191.9 2.8 %fusion.48 = f32[8,512,128]{2,1,0:T(8,128)} fusion(bf16[8,512,512]{2,1,0:T(8,128)(2,1)S(1)} %copy-done.1, bf16[512,8,128]{2,1,0:T(8,128)(2,1)S(1)} %copy-done.2), kind=kOutput, calls=%fused_computation.67 | convolution fusion | flops 536870912 | bytes 7340032 | tf_op jit(solution)/shard_map/hij,ihk->jhk/dot_general | solution.py:138
  194.8 2.5 %fusion.18 = f32[512,8,128]{0,2,1:T(8,128)} fusion(f32[8,512,3,128]{1,3,2,0:T(8,128)S(1)} %fusion.54, f32[3,512,8]{1,0,2:T(4,128)S(1)} %copy.148, bf16[512,8,128,1]{0,2,3,1:T(8,128)(2,1)S(1)} %copy.201, f32[3,8,128,128]{3,0,2,1:T(4,128)S(1)} %copy-done.4), kind=kOutput, calls=%fused_computation.25 | convolution fusion | flops 408420352 | bytes 11059200 | tf_op jit(solution)/shard_map/jhkv,ihv->jihk/dot_general | solution.py:39
  197.3 1.3 convert_element_type.226
  198.6 1.2 copy-done.14
  199.7 1.0 fusion.98
  200.7 1.5 collective-permute-start.1
  202.3 2.2 copy.186
  204.6 2.9 %copy.168 = f32[512,8,128]{2,0,1:T(8,128)} copy(f32[512,8,128]{0,2,1:T(8,128)} %fusion.18) | data formatting | bytes 4194304 | tf_op jit(solution)/shard_map/reduce_sum | solution.py:135
  207.5 4.1 %fusion.31 = bf16[512,8,128]{2,0,1:T(8,128)(2,1)S(1)} fusion(f32[512,8,128]{2,0,1:T(8,128)} %copy.168, bf16[8,512,512]{2,1,0:T(8,128)(2,1)} %get-tuple-element.32, bf16[512,8,128]{2,1,0:T(8,128)(2,1)S(1)} %copy-done.9), kind=kOutput, calls=%fused_computation.41 | convolution fusion | flops 537919488 | bytes 8388608 | tf_op jit(solution)/shard_map/hij,jhk->ihk/dot_general | solution.py:132
  211.6 3.3 %collective-permute-done.1 = bf16[2,8,128,128]{2,3,0,1:T(8,128)(2,1)} collective-permute-done((bf16[2,8,128,128]{2,3,0,1:T(8,128)(2,1)}, bf16[2,8,128,128]{2,3,0,1:T(8,128)(2,1)}, u32[]{:S(2)}, u32[]{:S(2)}) %collective-permute-start.1) | collective-permute-done | bytes 524320 | tf_op jit(solution)/shard_map/ppermute | solution.py:16
  215.0 1.1 convert_element_type.229
  216.2 2.5 %collective-permute-start.2 = (bf16[1,8,128,128]{2,3,0,1:T(8,128)(2,1)S(1)}, bf16[1,8,128,128]{2,3,0,1:T(8,128)(2,1)S(1)}, u32[]{:S(2)}, u32[]{:S(2)}) collective-permute-start(bf16[1,8,128,128]{2,3,0,1:T(8,128)(2,1)S(1)} %get-tuple-element.37), channel_id=1, source_target_pairs={{0,16},{16,0},{4,20},{20,4},{8,24},{24,8},{12,28},{28,12},{1,17},{... | collective-permute-start | bytes 786440 | tf_op jit(solution)/shard_map/ppermute | solution.py:16
  219.4 1.6 copy.188
  221.0 1.2 slice_multiply_fusion.1
  222.3 8.0 %collective-permute-done.2 = bf16[1,8,128,128]{2,3,0,1:T(8,128)(2,1)S(1)} collective-permute-done((bf16[1,8,128,128]{2,3,0,1:T(8,128)(2,1)S(1)}, bf16[1,8,128,128]{2,3,0,1:T(8,128)(2,1)S(1)}, u32[]{:S(2)}, u32[]{:S(2)}) %collective-permute-start.2) | collective-permute-done | bytes 262176 | tf_op jit(solution)/shard_map/ppermute | solution.py:16
  231.3 1.5 fusion.43
  232.8 2.6 %copy.190 = bf16[512,8,128]{2,1,0:T(8,128)(2,1)} copy(bf16[512,8,128]{0,2,1:T(8,128)(2,1)} %fusion.43) | data formatting | bytes 2097152
  235.3 1.4 fusion.58
  237.3 1.6 copy.189
  (54 shorter events, 5.5 us)
Async XLA Ops:
  7.2 1.2 copy-start
  7.2 4.6 %copy-start.16 = (f32[13,8,512]{2,1,0:T(8,128)S(1)}, f32[13,8,512]{2,1,0:T(8,128)}, u32[]{:S(2)}) copy-start(f32[13,8,512]{2,1,0:T(8,128)} %param.9) | copy-start | bytes 638980
  7.2 55.9 %all-gather.6.cloned.1.call-start = ((), (), s32[]{:S(2)}) async-start(), calls=%async_computation.3 | async-start | bytes 2359296 | tf_op jit(solution)/shard_map/all_gather | solution.py:77
  11.0 86.7 %all-gather.4.cloned.1.call-start = ((), (), s32[]{:S(2)}) async-start(), calls=%async_computation.2 | async-start | bytes 5242880 | tf_op jit(solution)/shard_map/all_gather | solution.py:62
  11.7 227.2 %reduce-scatter.2.cloned.1.call-start = ((), (), s32[]{:S(2)}) async-start(), calls=%async_computation.1 | async-start | bytes 5242880 | tf_op jit(solution)/shard_map/reduce_scatter | solution.py:113
  12.9 1.3 copy-start.13
  14.2 4.8 %copy-start.2 = (bf16[512,8,128]{2,1,0:T(8,128)(2,1)S(1)}, bf16[512,8,128]{2,1,0:T(8,128)(2,1)}, u32[]{:S(2)}) copy-start(bf16[512,8,128]{2,1,0:T(8,128)(2,1)} %param.6) | copy-start | bytes 3145732
  66.2 1.3 copy-start.3
  109.9 4.6 %copy-start.7 = (bf16[512,8,128]{0,2,1:T(8,128)(2,1)}, bf16[512,8,128]{0,2,1:T(8,128)(2,1)S(1)}, u32[]{:S(2)}) copy-start(bf16[512,8,128]{0,2,1:T(8,128)(2,1)S(1)} %copy.181) | copy-start | bytes 3145732
  154.2 6.4 %copy-start.5 = (f32[8,512,128]{2,1,0:T(8,128)S(1)}, f32[8,512,128]{2,1,0:T(8,128)}, u32[]{:S(2)}) copy-start(f32[8,512,128]{2,1,0:T(8,128)} %copy.172) | copy-start | bytes 6291460
  160.6 5.1 %copy-start.6 = (bf16[8,512,512]{2,1,0:T(8,128)(2,1)S(1)}, bf16[8,512,512]{2,1,0:T(8,128)(2,1)}, u32[]{:S(2)}) copy-start(bf16[8,512,512]{2,1,0:T(8,128)(2,1)} %get-tuple-element.33) | copy-start | bytes 12582916
  160.6 5.1 %copy-start.8 = (bf16[512,8,128]{0,2,1:T(8,128)(2,1)S(1)}, bf16[512,8,128]{0,2,1:T(8,128)(2,1)}, u32[]{:S(2)}) copy-start(bf16[512,8,128]{0,2,1:T(8,128)(2,1)} %copy-done.7) | copy-start | bytes 3145732
  164.2 3.6 %copy-start.4 = (f32[3,8,128,128]{3,0,2,1:T(4,128)S(1)}, f32[3,8,128,128]{3,0,2,1:T(4,128)}, u32[]{:S(2)}) copy-start(f32[3,8,128,128]{3,0,2,1:T(4,128)} %copy-done.3) | copy-start | bytes 4718596
  164.2 33.1 %collective-permute-start = (bf16[3,8,128,128]{2,3,0,1:T(8,128)(2,1)}, bf16[3,8,128,128]{2,3,0,1:T(8,128)(2,1)}, u32[]{:S(2)}, u32[]{:S(2)}) collective-permute-start(bf16[3,8,128,128]{2,3,0,1:T(8,128)(2,1)} %get-tuple-element.38), channel_id=1, source_target_pairs={{0,4},{4,0},{8,12},{12,8},{16,20},{20,16},{24,28},{28,24},{1,5},{5... | collective-permute-start | bytes 2359304 | tf_op jit(solution)/shard_map/ppermute | solution.py:16
  165.7 4.2 %copy-start.10 = (f32[8,512,512]{2,1,0:T(8,128)S(1)}, f32[8,512,512]{2,1,0:T(8,128)}, u32[]{:S(2)}) copy-start(f32[8,512,512]{2,1,0:T(8,128)} %get-tuple-element.31) | copy-start | bytes 25165828
  169.9 22.0 %copy-start.1 = (bf16[8,512,512]{2,1,0:T(8,128)(2,1)S(1)}, bf16[8,512,512]{2,1,0:T(8,128)(2,1)}, u32[]{:S(2)}) copy-start(bf16[8,512,512]{2,1,0:T(8,128)(2,1)} %get-tuple-element.32) | copy-start | bytes 12582916
  198.6 1.2 copy-start.14
  200.7 6.8 %copy-start.9 = (bf16[512,8,128]{2,1,0:T(8,128)(2,1)S(1)}, bf16[512,8,128]{2,1,0:T(8,128)(2,1)}, u32[]{:S(2)}) copy-start(bf16[512,8,128]{2,1,0:T(8,128)(2,1)} %param.7) | copy-start | bytes 3145732
  200.7 14.2 %collective-permute-start.1 = (bf16[2,8,128,128]{2,3,0,1:T(8,128)(2,1)}, bf16[2,8,128,128]{2,3,0,1:T(8,128)(2,1)}, u32[]{:S(2)}, u32[]{:S(2)}) collective-permute-start(bf16[2,8,128,128]{2,3,0,1:T(8,128)(2,1)} %get-tuple-element.29), channel_id=1, source_target_pairs={{0,8},{8,0},{4,12},{12,4},{16,24},{24,16},{20,28},{28,20},{1,9},{9... | collective-permute-start | bytes 1572872 | tf_op jit(solution)/shard_map/ppermute | solution.py:16
  216.2 14.0 %collective-permute-start.2 = (bf16[1,8,128,128]{2,3,0,1:T(8,128)(2,1)S(1)}, bf16[1,8,128,128]{2,3,0,1:T(8,128)(2,1)S(1)}, u32[]{:S(2)}, u32[]{:S(2)}) collective-permute-start(bf16[1,8,128,128]{2,3,0,1:T(8,128)(2,1)S(1)} %get-tuple-element.37), channel_id=1, source_target_pairs={{0,16},{16,0},{4,20},{20,4},{8,24},{24,8},{12,28},{28,12},{1,17},{... | collective-permute-start | bytes 786440 | tf_op jit(solution)/shard_map/ppermute | solution.py:16
  221.0 10.2 %copy-start.11 = (f32[8,128,512]{2,1,0:T(8,128)S(1)}, f32[8,128,512]{2,1,0:T(8,128)}, u32[]{:S(2)}) copy-start(f32[8,128,512]{2,1,0:T(8,128)} %fusion.102) | copy-start | bytes 6291460
  230.5 0.7 copy-start.15
  232.8 4.0 %copy-start.12 = (f32[8,512,128]{2,1,0:T(8,128)S(1)}, f32[8,512,128]{2,1,0:T(8,128)}, u32[]{:S(2)}) copy-start(f32[8,512,128]{2,1,0:T(8,128)} %fusion.48) | copy-start | bytes 6291460
Sparse Core Ops, SparseCore 0:
  11.1 51.9 all-gather.5
  64.7 32.9 all-gather.3
  154.3 44.5 reduce-scatter.1
where the time goes:
time: 250 us; the launch traced here: 246 us
  matrix products  123 us (49%)
  waiting for transfers between devices  60.4 us (24%)
  local copies, waits for them, and re-layouts  34.8 us (14%)
  between operations  14.5 us (6%)
  other arithmetic  7.74 us (3%)
  starting transfers between devices  5.61 us (2%)
    all_gather x1, waiting for transfers between devices, on_device(): lax.all_gather(grad_out, 'head', axis=1, tiled=True)  26.4 us
    dot_general x1, matrix products, on_device(): jnp.einsum('ilj,hij->lhi', onehot, scores * back, precision=PRECISE_MATCH)  22 us
    all_gather x1, waiting for transfers between devices, on_device(): lax.all_gather(key_weighted[None].astype(jnp.bfloat16), 'seq', axis=0, ti...  21.9 us
    dot_general x1, matrix products, on_device(): jnp.einsum('ilj,lhi->hij', onehot, weighted_levels[:near_levels], precisi...  18 us
    unnamed x39, local copies, waits for them, and re-layouts  14.3 us
    dot_general x1, matrix products, on_device(): jnp.einsum('ihk,jhk->hij', queries, key_matrix, preferred_element_type=jn...  13.8 us
    dot_general x1, matrix products, on_device(): lax.dot_general(columns, flat_att, (((0,), (1,)), ((), ())), preferred_el...  12.4 us
    ppermute x3, waiting for transfers between devices, partner_2(): return lax.ppermute(block, axis, route)  11.3 us
  transfers between devices with their start and end apart: 6, of which 4 were waited for; matrix products, arithmetic and copies ran while one was open for 41% of the time, Pallas kernels for 0%

commit v1 on v0

v1 whole, which is shorter than its diff:
```python
import math

import jax
import jax.numpy as jnp
from jax import lax
from jax.experimental import pallas as pl
from jax.experimental.pallas import tpu as pltpu
from jax.sharding import PartitionSpec as P

F32 = jnp.float32
BF16 = jnp.bfloat16
TILE = 128
CHUNKS = 2


def nn(a, b):
    return jnp.dot(a, b, preferred_element_type=F32)


def nt(a, b):
    return lax.dot_general(a, b, (((1,), (1,)), ((), ())), preferred_element_type=F32)


def make_kernel(T, NH, HD, L, D, FS, n_seq, n_head):
    far = n_seq.bit_length() - 1
    near = L - far
    nx = n_head // 2
    nb = T // TILE
    H = T // 2
    R = T // CHUNKS
    tile_levels = TILE.bit_length()
    c = [2.0 ** (-max(l - 1, 0) / 2) / math.sqrt(HD) for l in range(L)]
    tri = [sum(far - i for i in range(b)) for b in range(far)]
    n_sems = 1 + 2 * (nx - 1) * CHUNKS + far + far + (nx - 1) * CHUNKS * 2 + 1

    def kernel(q_hbm, k_hbm, v_hbm, lw_hbm, w_hbm, g_hbm,
               mo, dq, dk, dv, gl,
               q, k, v, lw, w, gall, vt, qt, lev, at, mix, ds, att_t, att, acc,
               dot_, do, s_send, s_recv, s_pend, f_t, f_n, p_send, p_recv, p_pend,
               r_sum, dkl, dvl, sib_send, sib_recv, x_send, x_recv, own,
               ssem, rsem, lsem):
        sid = lax.axis_index("seq")
        hid = lax.axis_index("head")
        chip = lax.div(hid, 2)
        core = lax.rem(hid, 2)
        other = 1 - core
        sib = {"head": chip * 2 + other}

        def chip_at(d):
            return lax.rem(chip + d, nx)

        def chip_from(d):
            return lax.rem(chip + nx - d, nx)

        def bit(b):
            return lax.rem(lax.div(sid, 2**b), 2)

        def seq_peer(b):
            return {"seq": sid + 2**b * (1 - 2 * bit(b))}

        x_to = [None] + [{"head": chip_at(d) * 2 + core} for d in range(1, nx)]
        peers = [sib] + [seq_peer(b) for b in range(far)]

        used = [0]

        def remote(src, dst, dev):
            i = used[0]
            used[0] += 1
            return pltpu.make_async_remote_copy(
                src_ref=src, dst_ref=dst, send_sem=ssem.at[i], recv_sem=rsem.at[i],
                device_id=dev, device_id_type=pl.DeviceIdType.MESH,
            )

        loads = [
            pltpu.make_async_copy(a, b, lsem.at[i])
            for i, (a, b) in enumerate(
                [(k_hbm, k), (v_hbm, v), (q_hbm, q), (lw_hbm, lw), (g_hbm, gall.at[0]), (w_hbm, w)]
            )
        ]
        for copy in loads:
            copy.start()

        barrier = pltpu.get_barrier_semaphore()
        for dev in peers + x_to[1:]:
            pl.semaphore_signal(barrier, inc=1, device_id=dev, device_id_type=pl.DeviceIdType.MESH)
        pl.semaphore_wait(barrier, len(peers) + nx - 1)

        ag_x = {}
        for part in range(CHUNKS):
            rows = pl.ds(part * R, R)
            for d in range(1, nx):
                ag_x[d, part] = remote(g_hbm.at[rows], gall.at[2 * d, rows], x_to[d])
                ag_x[d, part].start()
        ag_sib = remote(g_hbm, gall.at[1], sib)
        ag_sib.start()

        loads[0].wait()
        loads[1].wait()

        def outer(h, _):
            turned = v[h].T
            vt[h] = turned
            state = nn(turned, k[h])
            s_pend[h] = state
            s_send[0, h] = state.astype(BF16)
            return 0

        lax.fori_loop(0, NH, outer, 0)
        s_copy = []
        s_copy.append(remote(s_send.at[0], s_recv.at[0], seq_peer(0)))
        s_copy[0].start()

        rows_i = lax.broadcasted_iota(jnp.int32, (TILE, TILE), 0)
        cols_i = lax.broadcasted_iota(jnp.int32, (TILE, TILE), 1)
        gap = jnp.zeros((TILE, TILE), jnp.int32)
        for e in range(tile_levels - 1):
            gap = gap + (jnp.bitwise_xor(rows_i, cols_i) >= 2**e).astype(jnp.int32)
        lev[...] = jnp.where(rows_i <= cols_i, gap, -1)

        def blank(h, _):
            for bj in range(nb):
                for bi in range(bj):
                    at[h, pl.ds(bj * TILE, TILE), pl.ds(bi * TILE, TILE)] = jnp.zeros((TILE, TILE), BF16)
            return 0

        lax.fori_loop(0, NH, blank, 0)
        for bj in range(nb):
            for bi in range(bj):
                ds[pl.ds(bj * TILE, TILE), pl.ds(bi * TILE, TILE)] = jnp.zeros((TILE, TILE), BF16)
        loads[2].wait()
        loads[3].wait()

        def weight(l, h):
            return lw[l, pl.ds(h, 1), :] * c[l]

        def block(b):
            return slice(b * TILE, (b + 1) * TILE)

        def tile_of(top, bottom, bj, bi):
            if bj * TILE < H:
                return top[block(bj), block(bi)]
            return bottom[bj * TILE - H:(bj + 1) * TILE - H, bi * TILE - H:(bi + 1) * TILE - H]

        def level_of(bj, bi):
            return (bj ^ bi).bit_length() + tile_levels - 1

        def forward(h, _):
            kh, qh = k[h], q[h]
            qt[h] = qh.T
            top = nt(kh[:H], qh)
            bottom = nt(kh[H:], qh[H:])
            ws = [weight(l, h) for l in range(near)]
            for bi in range(nb):
                m = jnp.zeros((TILE, TILE), F32)
                for l in range(tile_levels):
                    m = jnp.where(lev[...] == l, ws[l][:, block(bi)], m)
                mix[h, bi] = m
                for bj in range(bi + 1):
                    t = tile_of(top, bottom, bj, bi)
                    factor = m if bi == bj else ws[level_of(bj, bi)][:, block(bi)]
                    at[h, pl.ds(bj * TILE, TILE), pl.ds(bi * TILE, TILE)] = (t * factor).astype(BF16)
            vth = vt[h]
            att_t[h, :, :H] = nn(vth[:, :H], at[h, :H, :H])
            att_t[h, :, H:] = nn(vth, at[h, :, H:])
            return 0

        def take_state(b):
            s_copy[b].wait()
            keep = bit(b).astype(F32)

            def body(h, _):
                got = s_recv[b, h].astype(F32)
                f = got * keep
                f_t[b, h] = f.astype(BF16)
                f_n[b, h] = f.T.astype(BF16)
                if b + 1 < far:
                    total = s_pend[h] + got
                    s_pend[h] = total
                    s_send[b + 1, h] = total.astype(BF16)
                return 0

            lax.fori_loop(0, NH, body, 0)
            if b + 1 < far:
                s_copy.append(remote(s_send.at[b + 1], s_recv.at[b + 1], seq_peer(b + 1)))
                s_copy[b + 1].start()

        fwd_copy = {}

        def pass_on(part):
            rows = pl.ds(part * R, R)
            for d in range(1, nx):
                ag_x[d, part].wait_recv()
                fwd_copy[d, part] = remote(gall.at[2 * d, rows], gall.at[2 * d + 1, rows], sib)
                fwd_copy[d, part].start()

        lax.fori_loop(0, NH // 2, forward, 0)
        take_state(0)
        lax.fori_loop(NH // 2, NH, forward, 0)
        for b in range(1, far - 1):
            take_state(b)
        pass_on(0)
        loads[4].wait()
        loads[5].wait()

        MB = min(256, NH * HD)

        def add_mix(slot, src, part, first, last):
            cols = pl.ds(pl.multiple_of(src * FS, FS), FS)

            def body(i, _):
                hd = pl.ds(pl.multiple_of(i * MB, MB), MB)
                lanes = pl.ds(part * R, R)
                term = nt(w[hd, cols], gall[slot, part * R:(part + 1) * R])
                if not first:
                    term = term + acc[hd, lanes]
                acc[hd, lanes] = term
                return 0

            lax.fori_loop(0, NH * HD // MB, body, 0)

        for part in range(CHUNKS):
            add_mix(0, hid, part, True, False)
        ag_sib.wait_recv()
        for part in range(CHUNKS):
            add_mix(1, chip * 2 + other, part, False, False)
        if far > 1:
            take_state(far - 1)

        def reads(h, _):
            qth = qt[h].astype(F32)
            left = jnp.concatenate([f_t[b, h] for b in range(far)], axis=1)
            right = jnp.concatenate([(qth * weight(near + b, h)).astype(BF16) for b in range(far)], axis=0)
            total = att_t[h] + nn(left, right)
            att[:, pl.ds(pl.multiple_of(h * HD, HD), HD)] = total.T.astype(BF16)
            return 0

        lax.fori_loop(0, NH, reads, 0)

        NB = min(256, FS)

        def project(dst, slot, dest, part):
            rows = slice(part * R, (part + 1) * R)

            def body(i, _):
                lanes = pl.ds(pl.multiple_of(i * NB, NB), NB)
                cols = pl.ds(pl.multiple_of(dest * FS + i * NB, NB), NB)
                dst[slot, rows, lanes] = nn(att[rows], w[:, cols]).astype(BF16)
                return 0

            lax.fori_loop(0, FS // NB, body, 0)

        sib_copy = {}
        for part in range(CHUNKS):
            rows = pl.ds(part * R, R)
            for d in range(1, nx):
                project(sib_send, d, chip_at(d) * 2 + other, part)
                sib_copy[d, part] = remote(sib_send.at[d, rows], sib_recv.at[d, rows], sib)
                sib_copy[d, part].start()
        for part in range(1, CHUNKS):
            pass_on(part)
        x_copy = {}
        for part in range(CHUNKS):
            rows = pl.ds(part * R, R)
            for d in range(1, nx):
                project(own, d, chip_at(d) * 2 + core, part)
                sib_copy[d, part].wait_recv()
                x_send[d - 1, rows] = (own[d, rows].astype(F32) + sib_recv[d, rows].astype(F32)).astype(BF16)
                x_copy[d, part] = remote(x_send.at[d - 1, rows], x_recv.at[d - 1, rows], x_to[d])
                x_copy[d, part].start()

        for part in range(CHUNKS):
            for d in range(1, nx):
                add_mix(2 * d, chip_from(d) * 2 + core, part, False, False)
            for d in range(1, nx):
                fwd_copy[d, part].wait_recv()
                add_mix(2 * d + 1, chip_from(d) * 2 + other, part, False, False)

        def back_state(h, _):
            turned = acc[pl.ds(pl.multiple_of(h * HD, HD), HD), :]
            dot_[h] = turned.astype(BF16)
            doh = turned.T.astype(BF16)
            do[h] = doh
            qth = qt[h].astype(F32)
            for b in range(far):
                state = nn((qth * weight(near + b, h)).astype(BF16), doh)
                p_pend[b, h] = state
                p_send[b, h] = state.astype(BF16)
            return 0

        lax.fori_loop(0, NH, back_state, 0)
        p_copy = []

        def send_back(b):
            part = pl.ds(tri[b], far - b)
            p_copy.append(remote(p_send.at[part], p_recv.at[part], seq_peer(b)))
            p_copy[b].start()

        def take_back(b):
            p_copy[b].wait()
            keep = 1.0 - bit(b).astype(F32)

            def body(h, _):
                got = p_recv[tri[b], h].astype(F32) * keep
                r_sum[h] = got if b == 0 else r_sum[h] + got
                for j in range(1, far - b):
                    total = p_pend[b + j, h] + p_recv[tri[b] + j, h].astype(F32)
                    p_pend[b + j, h] = total
                    p_send[tri[b + 1] + j - 1, h] = total.astype(BF16)
                return 0

            lax.fori_loop(0, NH, body, 0)
            if b + 1 < far:
                send_back(b + 1)

        send_back(0)

        def backward(h, _):
            kh, qh, vh = k[h], q[h], v[h]
            doth, doh = dot_[h], do[h]
            s_top = nt(kh[:H], qh)
            s_bottom = nt(kh[H:], qh[H:])
            b_top = nn(vh[:H], doth)
            b_bottom = nn(vh[H:], doth[:, H:])
            ws = [weight(l, h) for l in range(near)]
            sums = [[] for _ in range(near)]
            for bi in range(nb):
                far_sums = {}
                for bj in range(bi + 1):
                    back = tile_of(b_top, b_bottom, bj, bi)
                    product = tile_of(s_top, s_bottom, bj, bi) * back
                    if bi == bj:
                        factor = mix[h, bi]
                        for l in range(tile_levels):
                            sums[l].append(
                                jnp.sum(jnp.where(lev[...] == l, product, 0.0), axis=0, keepdims=True)
                            )
                    else:
                        l = level_of(bj, bi)
                        factor = ws[l][:, block(bi)]
                        far_sums[l] = far_sums[l] + product if l in far_sums else product
                    ds[pl.ds(bj * TILE, TILE), pl.ds(bi * TILE, TILE)] = (back * factor).astype(BF16)
                for l in range(tile_levels, near):
                    if l in far_sums:
                        sums[l].append(jnp.sum(far_sums[l], axis=0, keepdims=True))
                    else:
                        sums[l].append(jnp.zeros((1, TILE), F32))
            for l in range(near):
                gl[l, pl.ds(h, 1), :] = jnp.concatenate(sums[l], axis=1) * c[l]
            dvl[h, :H] = nn(at[h, :H, :], doh)
            dvl[h, H:] = nn(at[h, H:, H:], doh[H:])
            dkl[h, :H] = nn(ds[:H, :], qh)
            dkl[h, H:] = nn(ds[H:, H:], qh[H:])
            kt = kh.T
            dqt = jnp.concatenate([nn(kt[:, :H], ds[:H, :H]), nn(kt, ds[:, H:])], axis=1)
            qth = qt[h].astype(F32)
            for b in range(far):
                u = nn(f_n[b, h], doth)
                gl[near + b, pl.ds(h, 1), :] = jnp.sum(u * qth, axis=0, keepdims=True) * c[near + b]
                dqt = dqt + u * weight(near + b, h)
            dq[h] = dqt.T.astype(BF16)
            return 0

        lax.fori_loop(0, NH // 2, backward, 0)
        take_back(0)
        lax.fori_loop(NH // 2, NH, backward, 0)
        for b in range(1, far - 1):
            take_back(b)
        for part in range(CHUNKS):
            project(sib_send, 0, chip * 2 + other, part)
        last_copy = remote(sib_send.at[0], sib_recv.at[0], sib)
        last_copy.start()
        for part in range(CHUNKS):
            project(own, 0, hid, part)
        last_copy.wait()
        for part in range(CHUNKS):
            rows = pl.ds(part * R, R)
            total = own[0, rows].astype(F32) + sib_recv[0, rows].astype(F32)
            for d in range(1, nx):
                x_copy[d, part].wait_recv()
                total = total + x_recv[d - 1, rows].astype(F32)
            mo[rows] = total.astype(BF16)
        if far > 1:
            take_back(far - 1)

        def finish(h, _):
            r = r_sum[h].astype(BF16)
            dk[h] = (dkl[h] + nt(v[h], r)).astype(BF16)
            dv[h] = (dvl[h] + nn(k[h], r)).astype(BF16)
            return 0

        lax.fori_loop(0, NH, finish, 0)
        ag_sib.wait_send()
        for group in (ag_x, fwd_copy, sib_copy, x_copy):
            for copy in group.values():
                copy.wait_send()

    tri_total = far * (far + 1) // 2
    V = pltpu.VMEM
    scratch = [
        V((NH, T, HD), BF16), V((NH, T, HD), BF16), V((NH, T, HD), BF16), V((L, NH, T), F32),
        V((NH * HD, D), BF16), V((n_head, T, FS), BF16),
        V((NH, HD, T), BF16), V((NH, HD, T), BF16), V((TILE, TILE), jnp.int32),
        V((NH, T, T), BF16), V((NH, nb, TILE, TILE), F32), V((T, T), BF16),
        V((NH, HD, T), F32), V((T, NH * HD), BF16), V((NH * HD, T), F32),
        V((NH, HD, T), BF16), V((NH, T, HD), BF16),
        V((far, NH, HD, HD), BF16), V((far, NH, HD, HD), BF16), V((NH, HD, HD), F32),
        V((far, NH, HD, HD), BF16), V((far, NH, HD, HD), BF16),
        V((tri_total, NH, HD, HD), BF16), V((tri_total, NH, HD, HD), BF16), V((far, NH, HD, HD), F32),
        V((NH, HD, HD), F32), V((NH, T, HD), F32), V((NH, T, HD), F32),
        V((nx, T, FS), BF16), V((nx, T, FS), BF16), V((nx - 1, T, FS), BF16), V((nx - 1, T, FS), BF16),
        V((nx, T, FS), BF16),
        pltpu.SemaphoreType.DMA((n_sems,)), pltpu.SemaphoreType.DMA((n_sems,)),
        pltpu.SemaphoreType.DMA((6,)),
    ]
    return kernel, scratch


def solution(mesh):
    n_seq, n_head = mesh.shape["seq"], mesh.shape["head"]

    def on_device(queries, key_matrix, value_matrix, level_weight, out_weight, grad_out):
        T, NH, HD = queries.shape
        L = level_weight.shape[0]
        D = out_weight.shape[2]
        FS = grad_out.shape[1]
        kernel, scratch = make_kernel(T, NH, HD, L, D, FS, n_seq, n_head)
        heads_first = [jnp.swapaxes(a, 0, 1) for a in (queries, key_matrix, value_matrix)]
        mo, dq, dk, dv, gl = pl.pallas_call(
            kernel,
            out_shape=(
                jax.ShapeDtypeStruct((T, FS), BF16),
                jax.ShapeDtypeStruct((NH, T, HD), BF16),
                jax.ShapeDtypeStruct((NH, T, HD), BF16),
                jax.ShapeDtypeStruct((NH, T, HD), BF16),
                jax.ShapeDtypeStruct((L, NH, T), F32),
            ),
            in_specs=[pl.BlockSpec(memory_space=pl.ANY)] * 6,
            out_specs=tuple([pl.BlockSpec(memory_space=pltpu.VMEM)] * 5),
            scratch_shapes=scratch,
            compiler_params=pltpu.CompilerParams(
                collective_id=0, has_side_effects=True, vmem_limit_bytes=62 * 1024 * 1024
            ),
        )(*heads_first, level_weight, out_weight.reshape(NH * HD, D), grad_out)
        return (mo, *[jnp.swapaxes(a, 0, 1) for a in (dq, dk, dv)], gl)

    return jax.shard_map(
        on_device,
        mesh=mesh,
        in_specs=(
            P("seq", "head", None),
            P("seq", "head", None),
            P("seq", "head", None),
            P(None, "head", "seq"),
            P("head", None, None),
            P("seq", "head"),
        ),
        out_specs=(
            P("seq", "head"),
            P("seq", "head", None),
            P("seq", "head", None),
            P("seq", "head", None),
            P(None, "head", "seq"),
        ),
        check_vma=False,
    )
```

time: 250 us -> 114 us (0.46); the launches traced: 246 us -> 114 us
  matrix products: 123 us -> 0 us
  Pallas kernels: 0 us -> 96.1 us
  waiting for transfers between devices: 60.4 us -> 0 us
  local copies, waits for them, and re-layouts: 34.8 us -> 17.2 us
  between operations: 14.5 us -> 0.65 us
  other arithmetic: 7.74 us -> 0 us
  starting transfers between devices: 5.61 us -> 0 us
    dot_general x21 -> x0, matrix products: 123 us -> none  [the longest x1 22 us: on_device(): jnp.einsum('ilj,hij->lhi', onehot, scores * back, precision=PRECISE_MATCH)]
    pallas_call x0 -> x1, Pallas kernels: none -> 96.1 us  [on_device(): pl.pallas_call(kernel, out_shape=(jax.ShapeDtypeStruct((T, FS), BF16), ja...]
    all_gather x2 -> x0, waiting for transfers between devices: 48.3 us -> none  [the longest x1 26.4 us: on_device(): lax.all_gather(grad_out, 'head', axis=1, tiled=True)]
    ppermute x3 -> x0, waiting for transfers between devices: 11.3 us -> none  [partner_2(): return lax.ppermute(block, axis, route)]
    reduce_sum x2 -> x0, local copies, waits for them, and re-layouts: 5.81 us -> none  [the longest x1 2.91 us: on_device(): jnp.sum(far_rows * reads, axis=0)]
    ppermute x3 -> x0, starting transfers between devices: 5.49 us -> none  [partner_2(): return lax.ppermute(block, axis, route)]
    convert_element_type x4 -> x0, other arithmetic: 5.04 us -> none  [the longest x2 2.44 us: on_device(): partner_2(pending.astype(jnp.bfloat16), 'seq', bit_index)]
    slice x3 -> x0, local copies, waits for them, and re-layouts: 4.86 us -> none  [the longest x2 4.78 us: on_device(): far_weights = weighted_levels[near_levels:]]
  transfers between devices with their start and end apart: 6 -> 0, of which waited for: 4 -> 0; matrix products, arithmetic and copies ran while one was open for 41% -> 0% of each run, Pallas kernels for 0% -> 0%
where the time goes in v1:
time: 114 us
  Pallas kernels  96.1 us (84%)
  local copies, waits for them, and re-layouts  17.2 us (15%)
    pallas_call x1, Pallas kernels, on_device(): pl.pallas_call(kernel, out_shape=(jax.ShapeDtypeStruct((T, FS), BF16), ja...  96.1 us
    unnamed x8, local copies, waits for them, and re-layouts  13.9 us
    transpose x1, local copies, waits for them, and re-layouts, on_device(): jnp.swapaxes(a, 0, 1)  3.23 us

profile of v1, /device:TPU:0, one launch (start us, length us, event | category | flops | bytes accessed | tf_op | source)
XLA Modules:
  0.0 113.9 jit_solution(16821807522159255124)
XLA Ops:
  0.6 2.3 %copy.20 = bf16[512,8,128]{2,0,1:T(8,128)(2,1)} copy(bf16[512,8,128]{2,1,0:T(8,128)(2,1)} %param.6) | data formatting | bytes 2097152 | tf_op args[0]
  3.0 3.2 %copy_bitcast_fusion = (bf16[8,512,128]{2,1,0:T(8,128)(2,1)}, bf16[8,512,128]{2,1,0:T(8,128)(2,1)}) fusion(bf16[512,8,128]{2,1,0:T(8,128)(2,1)} %param.8, bf16[512,8,128]{2,1,0:T(8,128)(2,1)} %param.7), kind=kLoop, calls=%fused_computation | loop fusion | bytes 4194304 | tf_op jit(solution)/shard_map/transpose | solution.py:427
  6.2 96.1 %shard_map.101 = (bf16[512,1024]{1,0:T(8,128)(2,1)}, bf16[8,512,128]{2,1,0:T(8,128)(2,1)}, bf16[8,512,128]{2,1,0:T(8,128)(2,1)}, bf16[8,512,128]{2,1,0:T(8,128)(2,1)}, f32[13,8,512]{2,1,0:T(8,128)}) custom-call(bf16[8,512,128]{2,1,0:T(8,128)(2,1)} %bitcast.12, bf16[8,512,128]{2,1,0:T(8,128)(2,1)} %get-tuple-element.21.k_hbm, ...), custom_call_target="tpu_custom_call" | custom-call | tf_op jit(solution)/shard_map/pallas_call | solution.py:428
  102.3 0.0 copy-start
  102.3 2.9 %copy.14 = bf16[512,8,128]{2,1,0:T(8,128)(2,1)} copy(bf16[512,8,128]{2,0,1:T(8,128)(2,1)} %bitcast.15) | data formatting | bytes 2097152
  105.2 2.9 %copy.15 = bf16[512,8,128]{2,1,0:T(8,128)(2,1)} copy(bf16[512,8,128]{2,0,1:T(8,128)(2,1)} %bitcast.14) | data formatting | bytes 2097152
  108.1 2.9 %copy.16 = bf16[512,8,128]{2,1,0:T(8,128)(2,1)} copy(bf16[512,8,128]{2,0,1:T(8,128)(2,1)} %bitcast.13) | data formatting | bytes 2097152
  111.0 2.3 %copy.23 = bf16[512,1024]{1,0:T(8,128)(2,1)} copy(bf16[512,1024]{1,0:T(8,128)(2,1)} %get-tuple-element.27) | data formatting | bytes 2097152
  113.2 0.0 copy-done
  113.2 0.7 copy.24
Async XLA Ops:
  102.3 10.9 %copy-start = (f32[13,8,512]{2,1,0:T(8,128)S(1)}, f32[13,8,512]{2,1,0:T(8,128)}, u32[]{:S(2)}) copy-start(f32[13,8,512]{2,1,0:T(8,128)} %get-tuple-element.31) | copy-start | bytes 638980

commit v2 on v1

--- a/solution.py
+++ b/solution.py
@@ -31,14 +31,14 @@
     tile_levels = TILE.bit_length()
     c = [2.0 ** (-max(l - 1, 0) / 2) / math.sqrt(HD) for l in range(L)]
     tri = [sum(far - i for i in range(b)) for b in range(far)]
-    n_sems = 1 + 2 * (nx - 1) * CHUNKS + far + far + (nx - 1) * CHUNKS * 2 + 1
+    n_sems = 1 + 2 * (nx - 1) * CHUNKS + far + far * (far + 1) // 2 + (nx - 1) * CHUNKS * 2 + 1
 
     def kernel(q_hbm, k_hbm, v_hbm, lw_hbm, w_hbm, g_hbm,
                mo, dq, dk, dv, gl,
                q, k, v, lw, w, gall, vt, qt, lev, at, mix, ds, att_t, att, acc,
                dot_, do, s_send, s_recv, s_pend, f_t, f_n, p_send, p_recv, p_pend,
                r_sum, dkl, dvl, sib_send, sib_recv, x_send, x_recv, own,
-               ssem, rsem, lsem):
+               raw, ssem, rsem, lsem):
         sid = lax.axis_index("seq")
         hid = lax.axis_index("head")
         chip = lax.div(hid, 2)
@@ -74,10 +74,10 @@
         loads = [
             pltpu.make_async_copy(a, b, lsem.at[i])
             for i, (a, b) in enumerate(
-                [(k_hbm, k), (v_hbm, v), (q_hbm, q), (lw_hbm, lw), (g_hbm, gall.at[0]), (w_hbm, w)]
+                [(k_hbm, raw.at[0]), (v_hbm, raw.at[1]), (lw_hbm, lw), (g_hbm, gall.at[0]), (w_hbm, w), (q_hbm, raw.at[0])]
             )
         ]
-        for copy in loads:
+        for copy in loads[:-1]:
             copy.start()
 
         barrier = pltpu.get_barrier_semaphore()
@@ -94,8 +94,19 @@
         ag_sib = remote(g_hbm, gall.at[1], sib)
         ag_sib.start()
 
+        def by_head(slot, dst):
+            def body(i, _):
+                rows = pl.ds(pl.multiple_of(i * TILE, TILE), TILE)
+                dst[:, rows, :] = jnp.swapaxes(raw[slot, rows], 0, 1)
+                return 0
+
+            lax.fori_loop(0, T // TILE, body, 0)
+
         loads[0].wait()
+        by_head(0, k)
+        loads[5].start()
         loads[1].wait()
+        by_head(1, v)
 
         def outer(h, _):
             turned = v[h].T
@@ -128,7 +139,8 @@
             for bi in range(bj):
                 ds[pl.ds(bj * TILE, TILE), pl.ds(bi * TILE, TILE)] = jnp.zeros((TILE, TILE), BF16)
         loads[2].wait()
-        loads[3].wait()
+        loads[5].wait()
+        by_head(0, q)
 
         def weight(l, h):
             return lw[l, pl.ds(h, 1), :] * c[l]
@@ -199,8 +211,8 @@
         for b in range(1, far - 1):
             take_state(b)
         pass_on(0)
+        loads[3].wait()
         loads[4].wait()
-        loads[5].wait()
 
         MB = min(256, NH * HD)
 
@@ -275,44 +287,55 @@
                 fwd_copy[d, part].wait_recv()
                 add_mix(2 * d + 1, chip_from(d) * 2 + other, part, False, False)
 
-        def back_state(h, _):
+        def mix_grad(h, _):
             turned = acc[pl.ds(pl.multiple_of(h * HD, HD), HD), :]
             dot_[h] = turned.astype(BF16)
-            doh = turned.T.astype(BF16)
-            do[h] = doh
-            qth = qt[h].astype(F32)
-            for b in range(far):
-                state = nn((qth * weight(near + b, h)).astype(BF16), doh)
-                p_pend[b, h] = state
-                p_send[b, h] = state.astype(BF16)
-            return 0
-
-        lax.fori_loop(0, NH, back_state, 0)
-        p_copy = []
-
-        def send_back(b):
-            part = pl.ds(tri[b], far - b)
-            p_copy.append(remote(p_send.at[part], p_recv.at[part], seq_peer(b)))
-            p_copy[b].start()
-
-        def take_back(b):
-            p_copy[b].wait()
+            do[h] = turned.T.astype(BF16)
+            return 0
+
+        lax.fori_loop(0, NH, mix_grad, 0)
+        p_copy = {}
+
+        def send_back(j, b):
+            i = tri[b] + j - b
+            p_copy[j, b] = remote(p_send.at[i], p_recv.at[i], seq_peer(b))
+            p_copy[j, b].start()
+
+        for j in reversed(range(far)):
+
+            def back_state(h, _):
+                scaled = (qt[h].astype(F32) * weight(near + j, h)).astype(BF16)
+                state = nn(scaled, do[h])
+                p_pend[j, h] = state
+                p_send[j, h] = state.astype(BF16)
+                return 0
+
+            lax.fori_loop(0, NH, back_state, 0)
+            send_back(j, 0)
+
+        started = []
+
+        def take_back(j, b):
+            p_copy[j, b].wait()
             keep = 1.0 - bit(b).astype(F32)
 
             def body(h, _):
-                got = p_recv[tri[b], h].astype(F32) * keep
-                r_sum[h] = got if b == 0 else r_sum[h] + got
-                for j in range(1, far - b):
-                    total = p_pend[b + j, h] + p_recv[tri[b] + j, h].astype(F32)
-                    p_pend[b + j, h] = total
-                    p_send[tri[b + 1] + j - 1, h] = total.astype(BF16)
+                got = p_recv[tri[b] + j - b, h].astype(F32)
+                if b < j:
+                    total = p_pend[j, h] + got
+                    p_pend[j, h] = total
+                    p_send[tri[b + 1] + j - b - 1, h] = total.astype(BF16)
+                elif started:
+                    r_sum[h] = r_sum[h] + got * keep
+                else:
+                    r_sum[h] = got * keep
                 return 0
 
             lax.fori_loop(0, NH, body, 0)
-            if b + 1 < far:
-                send_back(b + 1)
-
-        send_back(0)
+            if b < j:
+                send_back(j, b + 1)
+            else:
+                started.append(j)
 
         def backward(h, _):
             kh, qh, vh = k[h], q[h], v[h]
@@ -360,11 +383,18 @@
             dq[h] = dqt.T.astype(BF16)
             return 0
 
-        lax.fori_loop(0, NH // 2, backward, 0)
-        take_back(0)
-        lax.fori_loop(NH // 2, NH, backward, 0)
-        for b in range(1, far - 1):
-            take_back(b)
+        arrivals = [(j, b) for b in range(far) for j in reversed(range(b, far))]
+        early = [a for a in arrivals if a[1] == 0]
+        late = [a for a in arrivals if a[1] == far - 1]
+        cuts = [0, (3 * NH) // 8, (6 * NH) // 8, NH]
+        lax.fori_loop(cuts[0], cuts[1], backward, 0)
+        for j, b in early:
+            take_back(j, b)
+        lax.fori_loop(cuts[1], cuts[2], backward, 0)
+        for j, b in arrivals:
+            if (j, b) not in early and (j, b) not in late:
+                take_back(j, b)
+        lax.fori_loop(cuts[2], cuts[3], backward, 0)
         for part in range(CHUNKS):
             project(sib_send, 0, chip * 2 + other, part)
         last_copy = remote(sib_send.at[0], sib_recv.at[0], sib)
@@ -379,8 +409,9 @@
                 x_copy[d, part].wait_recv()
                 total = total + x_recv[d - 1, rows].astype(F32)
             mo[rows] = total.astype(BF16)
-        if far > 1:
-            take_back(far - 1)
+        for j, b in late:
+            if b > 0:
+                take_back(j, b)
 
         def finish(h, _):
             r = r_sum[h].astype(BF16)
@@ -408,11 +439,38 @@
         V((tri_total, NH, HD, HD), BF16), V((tri_total, NH, HD, HD), BF16), V((far, NH, HD, HD), F32),
         V((NH, HD, HD), F32), V((NH, T, HD), F32), V((NH, T, HD), F32),
         V((nx, T, FS), BF16), V((nx, T, FS), BF16), V((nx - 1, T, FS), BF16), V((nx - 1, T, FS), BF16),
-        V((nx, T, FS), BF16),
+        V((nx, T, FS), BF16), V((2, T, NH, HD), BF16),
         pltpu.SemaphoreType.DMA((n_sems,)), pltpu.SemaphoreType.DMA((n_sems,)),
         pltpu.SemaphoreType.DMA((6,)),
     ]
     return kernel, scratch
+
+
+def lay_out_kernel(mo, dq, dk, dv, gl, mo_out, dq_out, dk_out, dv_out, gl_out):
+    mo_out[...] = mo[...]
+    for a, b in ((dq, dq_out), (dk, dk_out), (dv, dv_out)):
+        b[...] = jnp.swapaxes(a[...], 0, 1)
+    gl_out[...] = gl[...]
+
+
+def lay_out(results, T, NH, HD, L, FS):
+    heads = pl.BlockSpec((NH, TILE, HD), lambda i: (0, i, 0))
+    tokens = pl.BlockSpec((TILE, NH, HD), lambda i: (i, 0, 0))
+    flat = pl.BlockSpec((TILE, FS), lambda i: (i, 0))
+    levels = pl.BlockSpec((L, NH, TILE), lambda i: (0, 0, i))
+    return pl.pallas_call(
+        lay_out_kernel,
+        grid=(T // TILE,),
+        out_shape=(
+            jax.ShapeDtypeStruct((T, FS), BF16),
+            jax.ShapeDtypeStruct((T, NH, HD), BF16),
+            jax.ShapeDtypeStruct((T, NH, HD), BF16),
+            jax.ShapeDtypeStruct((T, NH, HD), BF16),
+            jax.ShapeDtypeStruct((L, NH, T), F32),
+        ),
+        in_specs=[flat, heads, heads, heads, levels],
+        out_specs=(flat, tokens, tokens, tokens, levels),
+    )(*results)
 
 
 def solution(mesh):
@@ -424,8 +482,7 @@
         D = out_weight.shape[2]
         FS = grad_out.shape[1]
         kernel, scratch = make_kernel(T, NH, HD, L, D, FS, n_seq, n_head)
-        heads_first = [jnp.swapaxes(a, 0, 1) for a in (queries, key_matrix, value_matrix)]
-        mo, dq, dk, dv, gl = pl.pallas_call(
+        results = pl.pallas_call(
             kernel,
             out_shape=(
                 jax.ShapeDtypeStruct((T, FS), BF16),
@@ -440,8 +497,8 @@
             compiler_params=pltpu.CompilerParams(
                 collective_id=0, has_side_effects=True, vmem_limit_bytes=62 * 1024 * 1024
             ),
-        )(*heads_first, level_weight, out_weight.reshape(NH * HD, D), grad_out)
-        return (mo, *[jnp.swapaxes(a, 0, 1) for a in (dq, dk, dv)], gl)
+        )(queries, key_matrix, value_matrix, level_weight, out_weight.reshape(NH * HD, D), grad_out)
+        return lay_out(results, T, NH, HD, L, FS)
 
     return jax.shard_map(
         on_device,

time: 114 us -> 93.4 us (0.82)
  local copies, waits for them, and re-layouts: 17.2 us -> 0 us
  Pallas kernels: 96.1 us -> 92.5 us
    unnamed x8 -> x0, local copies, waits for them, and re-layouts: 13.9 us -> none
    pallas_call x1, Pallas kernels: 96.1 us -> 87.8 us  [on_device(): pl.pallas_call(kernel, out_shape=(jax.ShapeDtypeStruct((T, FS), BF16), ja...]
    pallas_call x0 -> x1, Pallas kernels: none -> 4.76 us  [lay_out(): pl.pallas_call(lay_out_kernel, grid=(T // TILE,), out_shape=(jax.ShapeDty...]
    transpose x1 -> x0, local copies, waits for them, and re-layouts: 3.23 us -> none  [on_device(): jnp.swapaxes(a, 0, 1)]
where the time goes in v2:
time: 93.4 us; the launch traced here: 93.2 us
  Pallas kernels  92.5 us (99%)
    pallas_call x1, Pallas kernels, on_device(): pl.pallas_call(kernel, out_shape=(jax.ShapeDtypeStruct((T, FS), BF16), ja...  87.8 us
    pallas_call x1, Pallas kernels, lay_out(): pl.pallas_call(lay_out_kernel, grid=(T // TILE,), out_shape=(jax.ShapeDty...  4.76 us

profile of v2, /device:TPU:0, one launch (start us, length us, event | category | flops | bytes accessed | tf_op | source)
XLA Modules:
  0.0 93.2 jit_solution(8947682565620659293)
XLA Ops:
  0.6 87.8 %shard_map.101 = (bf16[512,1024]{1,0:T(8,128)(2,1)}, bf16[8,512,128]{2,1,0:T(8,128)(2,1)}, bf16[8,512,128]{2,1,0:T(8,128)(2,1)}, bf16[8,512,128]{2,1,0:T(8,128)(2,1)}, f32[13,8,512]{2,1,0:T(8,128)}) custom-call(bf16[512,8,128]{2,1,0:T(8,128)(2,1)} %q_hbm.1, bf16[512,8,128]{2,1,0:T(8,128)(2,1)} %k_hbm.1, bf16[512,8,128]{2,1,0:T(8,128)(2,1)} %v_hbm.1, ...), custom_call_target="tpu_custom_call" | custom-call | tf_op jit(solution)/shard_map/pallas_call | solution.py:485
  88.4 4.8 %shard_map.102 = (bf16[512,1024]{1,0:T(8,128)(2,1)}, bf16[512,8,128]{2,1,0:T(8,128)(2,1)}, bf16[512,8,128]{2,1,0:T(8,128)(2,1)}, bf16[512,8,128]{2,1,0:T(8,128)(2,1)}, f32[13,8,512]{2,1,0:T(8,128)}) custom-call(bf16[512,1024]{1,0:T(8,128)(2,1)} %get-tuple-element.10.mo, bf16[8,512,128]{2,1,0:T(8,128)(2,1)} %get-tuple-element.11.dq, ...), custom_call_target="tpu_custom_call" | custom-call | tf_op jit(solution)/shard_map/pallas_call | solution.py:461

commit v3 on v2

--- a/solution.py
+++ b/solution.py
@@ -30,14 +30,13 @@
     R = T // CHUNKS
     tile_levels = TILE.bit_length()
     c = [2.0 ** (-max(l - 1, 0) / 2) / math.sqrt(HD) for l in range(L)]
-    tri = [sum(far - i for i in range(b)) for b in range(far)]
-    n_sems = 1 + 2 * (nx - 1) * CHUNKS + far + far * (far + 1) // 2 + (nx - 1) * CHUNKS * 2 + 1
+    n_sems = 1 + 2 * (nx - 1) * CHUNKS + far + far * (2 * far) + (nx - 1) * CHUNKS * 2 + 1
 
     def kernel(q_hbm, k_hbm, v_hbm, lw_hbm, w_hbm, g_hbm,
                mo, dq, dk, dv, gl,
                q, k, v, lw, w, gall, vt, qt, lev, at, mix, ds, att_t, att, acc,
                dot_, do, s_send, s_recv, s_pend, f_t, f_n, p_send, p_recv, p_pend,
-               r_sum, dkl, dvl, sib_send, sib_recv, x_send, x_recv, own,
+               p_done, dkl, dvl, sib_send, sib_recv, x_send, x_recv, own,
                raw, ssem, rsem, lsem):
         sid = lax.axis_index("seq")
         hid = lax.axis_index("head")
@@ -235,6 +234,99 @@
         ag_sib.wait_recv()
         for part in range(CHUNKS):
             add_mix(1, chip * 2 + other, part, False, False)
+        for part in range(CHUNKS):
+            if part > 0:
+                pass_on(part)
+            for d in range(1, nx):
+                add_mix(2 * d, chip_from(d) * 2 + core, part, False, False)
+            for d in range(1, nx):
+                fwd_copy[d, part].wait_recv()
+                add_mix(2 * d + 1, chip_from(d) * 2 + other, part, False, False)
+
+        def mix_grad(h, _):
+            turned = acc[pl.ds(pl.multiple_of(h * HD, HD), HD), :]
+            dot_[h] = turned.astype(BF16)
+            do[h] = turned.T.astype(BF16)
+            return 0
+
+        lax.fori_loop(0, NH, mix_grad, 0)
+        slots = [0]
+
+        def start_chain(j):
+            plan, count = [], NH
+            for b in range(j):
+                split = count % 2 == 0
+                plan.append((b, "sum", split))
+                count = count // 2 if split else count
+            plan.append((j, "last", False))
+            plan += [(b, "join", True) for b, _, split in reversed(plan[:-1]) if split]
+            return {"level": j, "plan": plan, "at": 0, "offset": sid * 0, "count": NH}
+
+        def send(chain):
+            j = chain["level"]
+            b, kind, split = chain["plan"][chain["at"]]
+            offset, count = chain["offset"], chain["count"]
+            if kind == "join":
+                part = pl.ds(offset, count)
+                copy = remote(p_done.at[j, part], p_done.at[j, part], seq_peer(b))
+            else:
+                half = count // 2 if split else count
+                first = offset + (1 - bit(b)) * half if split else offset
+                slot = slots[0]
+                slots[0] += half
+
+                def fill(i, _):
+                    p_send[slot + i] = p_pend[j, first + i].astype(BF16)
+                    return 0
+
+                lax.fori_loop(0, half, fill, 0)
+                source = p_send.at[pl.ds(slot, half)]
+                if kind == "last":
+                    copy = remote(source, p_done.at[j, pl.ds(offset, count)], seq_peer(b))
+                else:
+                    copy = remote(source, p_recv.at[pl.ds(slot, half)], seq_peer(b))
+                    chain["offset"] = offset + bit(b) * half if split else offset
+                    chain["count"] = half
+                    chain["slot"] = slot
+            copy.start()
+            chain["copy"] = copy
+
+        def advance(chain):
+            j = chain["level"]
+            b, kind, split = chain["plan"][chain["at"]]
+            chain["copy"].wait()
+            if kind == "sum":
+                slot, offset = chain["slot"], chain["offset"]
+
+                def add(i, _):
+                    p_pend[j, offset + i] = p_pend[j, offset + i] + p_recv[slot + i].astype(F32)
+                    return 0
+
+                lax.fori_loop(0, chain["count"], add, 0)
+            elif kind == "join":
+                chain["offset"] = chain["offset"] - bit(b) * chain["count"]
+                chain["count"] *= 2
+            chain["at"] += 1
+            if chain["at"] < len(chain["plan"]):
+                send(chain)
+
+        chains = []
+        for j in reversed(range(far)):
+
+            def back_state(h, _):
+                scaled = (qt[h].astype(F32) * weight(near + j, h)).astype(BF16)
+                p_pend[j, h] = nn(scaled, do[h])
+                return 0
+
+            lax.fori_loop(0, NH, back_state, 0)
+            chains.append(start_chain(j))
+            send(chains[-1])
+
+        def poll():
+            for chain in chains:
+                if chain["at"] < len(chain["plan"]):
+                    advance(chain)
+
         if far > 1:
             take_state(far - 1)
 
@@ -268,8 +360,7 @@
                 project(sib_send, d, chip_at(d) * 2 + other, part)
                 sib_copy[d, part] = remote(sib_send.at[d, rows], sib_recv.at[d, rows], sib)
                 sib_copy[d, part].start()
-        for part in range(1, CHUNKS):
-            pass_on(part)
+        poll()
         x_copy = {}
         for part in range(CHUNKS):
             rows = pl.ds(part * R, R)
@@ -280,62 +371,7 @@
                 x_copy[d, part] = remote(x_send.at[d - 1, rows], x_recv.at[d - 1, rows], x_to[d])
                 x_copy[d, part].start()
 
-        for part in range(CHUNKS):
-            for d in range(1, nx):
-                add_mix(2 * d, chip_from(d) * 2 + core, part, False, False)
-            for d in range(1, nx):
-                fwd_copy[d, part].wait_recv()
-                add_mix(2 * d + 1, chip_from(d) * 2 + other, part, False, False)
-
-        def mix_grad(h, _):
-            turned = acc[pl.ds(pl.multiple_of(h * HD, HD), HD), :]
-            dot_[h] = turned.astype(BF16)
-            do[h] = turned.T.astype(BF16)
-            return 0
-
-        lax.fori_loop(0, NH, mix_grad, 0)
-        p_copy = {}
-
-        def send_back(j, b):
-            i = tri[b] + j - b
-            p_copy[j, b] = remote(p_send.at[i], p_recv.at[i], seq_peer(b))
-            p_copy[j, b].start()
-
-        for j in reversed(range(far)):
-
-            def back_state(h, _):
-                scaled = (qt[h].astype(F32) * weight(near + j, h)).astype(BF16)
-                state = nn(scaled, do[h])
-                p_pend[j, h] = state
-                p_send[j, h] = state.astype(BF16)
-                return 0
-
-            lax.fori_loop(0, NH, back_state, 0)
-            send_back(j, 0)
-
-        started = []
-
-        def take_back(j, b):
-            p_copy[j, b].wait()
-            keep = 1.0 - bit(b).astype(F32)
-
-            def body(h, _):
-                got = p_recv[tri[b] + j - b, h].astype(F32)
-                if b < j:
-                    total = p_pend[j, h] + got
-                    p_pend[j, h] = total
-                    p_send[tri[b + 1] + j - b - 1, h] = total.astype(BF16)
-                elif started:
-                    r_sum[h] = r_sum[h] + got * keep
-                else:
-                    r_sum[h] = got * keep
-                return 0
-
-            lax.fori_loop(0, NH, body, 0)
-            if b < j:
-                send_back(j, b + 1)
-            else:
-                started.append(j)
+        poll()
 
         def backward(h, _):
             kh, qh, vh = k[h], q[h], v[h]
@@ -383,24 +419,28 @@
             dq[h] = dqt.T.astype(BF16)
             return 0
 
-        arrivals = [(j, b) for b in range(far) for j in reversed(range(b, far))]
-        early = [a for a in arrivals if a[1] == 0]
-        late = [a for a in arrivals if a[1] == far - 1]
         cuts = [0, (3 * NH) // 8, (6 * NH) // 8, NH]
         lax.fori_loop(cuts[0], cuts[1], backward, 0)
-        for j, b in early:
-            take_back(j, b)
+        poll()
         lax.fori_loop(cuts[1], cuts[2], backward, 0)
-        for j, b in arrivals:
-            if (j, b) not in early and (j, b) not in late:
-                take_back(j, b)
-        lax.fori_loop(cuts[2], cuts[3], backward, 0)
+        poll()
         for part in range(CHUNKS):
             project(sib_send, 0, chip * 2 + other, part)
         last_copy = remote(sib_send.at[0], sib_recv.at[0], sib)
         last_copy.start()
         for part in range(CHUNKS):
             project(own, 0, hid, part)
+        lax.fori_loop(cuts[2], cuts[3], backward, 0)
+        for _ in range(max(2 * far - 1 - 4, 0)):
+            poll()
+
+        def finish(h, _):
+            r = sum(p_done[j, h].astype(F32) * (1.0 - bit(j).astype(F32)) for j in range(far)).astype(BF16)
+            dk[h] = (dkl[h] + nt(v[h], r)).astype(BF16)
+            dv[h] = (dvl[h] + nn(k[h], r)).astype(BF16)
+            return 0
+
+        lax.fori_loop(0, NH, finish, 0)
         last_copy.wait()
         for part in range(CHUNKS):
             rows = pl.ds(part * R, R)
@@ -409,23 +449,18 @@
                 x_copy[d, part].wait_recv()
                 total = total + x_recv[d - 1, rows].astype(F32)
             mo[rows] = total.astype(BF16)
-        for j, b in late:
-            if b > 0:
-                take_back(j, b)
-
-        def finish(h, _):
-            r = r_sum[h].astype(BF16)
-            dk[h] = (dkl[h] + nt(v[h], r)).astype(BF16)
-            dv[h] = (dvl[h] + nn(k[h], r)).astype(BF16)
-            return 0
-
-        lax.fori_loop(0, NH, finish, 0)
         ag_sib.wait_send()
         for group in (ag_x, fwd_copy, sib_copy, x_copy):
             for copy in group.values():
                 copy.wait_send()
 
-    tri_total = far * (far + 1) // 2
+    slots_total = 0
+    for j in range(far):
+        count = NH
+        for _ in range(j):
+            count = count // 2 if count % 2 == 0 else count
+            slots_total += count
+        slots_total += count
     V = pltpu.VMEM
     scratch = [
         V((NH, T, HD), BF16), V((NH, T, HD), BF16), V((NH, T, HD), BF16), V((L, NH, T), F32),
@@ -436,8 +471,8 @@
         V((NH, HD, T), BF16), V((NH, T, HD), BF16),
         V((far, NH, HD, HD), BF16), V((far, NH, HD, HD), BF16), V((NH, HD, HD), F32),
         V((far, NH, HD, HD), BF16), V((far, NH, HD, HD), BF16),
-        V((tri_total, NH, HD, HD), BF16), V((tri_total, NH, HD, HD), BF16), V((far, NH, HD, HD), F32),
-        V((NH, HD, HD), F32), V((NH, T, HD), F32), V((NH, T, HD), F32),
+        V((slots_total, HD, HD), BF16), V((slots_total, HD, HD), BF16), V((far, NH, HD, HD), F32),
+        V((far, NH, HD, HD), BF16), V((NH, T, HD), F32), V((NH, T, HD), F32),
         V((nx, T, FS), BF16), V((nx, T, FS), BF16), V((nx - 1, T, FS), BF16), V((nx - 1, T, FS), BF16),
         V((nx, T, FS), BF16), V((2, T, NH, HD), BF16),
         pltpu.SemaphoreType.DMA((n_sems,)), pltpu.SemaphoreType.DMA((n_sems,)),

time: 93.4 us -> 83.5 us (0.89)
  Pallas kernels: 92.5 us -> 82.7 us
    pallas_call x1, Pallas kernels: 87.8 us -> 77.9 us  [on_device(): pl.pallas_call(kernel, out_shape=(jax.ShapeDtypeStruct((T, FS), BF16), ja...]
where the time goes in v3:
time: 83.5 us; the launch traced here: 83.3 us
  Pallas kernels  82.7 us (99%)
    pallas_call x1, Pallas kernels, on_device(): pl.pallas_call(kernel, out_shape=(jax.ShapeDtypeStruct((T, FS), BF16), ja...  77.9 us
    pallas_call x1, Pallas kernels, lay_out(): pl.pallas_call(lay_out_kernel, grid=(T // TILE,), out_shape=(jax.ShapeDty...  4.76 us

profile of v3, /device:TPU:0, one launch (start us, length us, event | category | flops | bytes accessed | tf_op | source)
XLA Modules:
  0.0 83.3 jit_solution(9443603841727116943)
XLA Ops:
  0.6 77.9 %shard_map.101 = (bf16[512,1024]{1,0:T(8,128)(2,1)}, bf16[8,512,128]{2,1,0:T(8,128)(2,1)}, bf16[8,512,128]{2,1,0:T(8,128)(2,1)}, bf16[8,512,128]{2,1,0:T(8,128)(2,1)}, f32[13,8,512]{2,1,0:T(8,128)}) custom-call(bf16[512,8,128]{2,1,0:T(8,128)(2,1)} %q_hbm.1, bf16[512,8,128]{2,1,0:T(8,128)(2,1)} %k_hbm.1, bf16[512,8,128]{2,1,0:T(8,128)(2,1)} %v_hbm.1, ...), custom_call_target="tpu_custom_call" | custom-call | tf_op jit(solution)/shard_map/pallas_call | solution.py:520
  78.6 4.8 %shard_map.102 = (bf16[512,1024]{1,0:T(8,128)(2,1)}, bf16[512,8,128]{2,1,0:T(8,128)(2,1)}, bf16[512,8,128]{2,1,0:T(8,128)(2,1)}, bf16[512,8,128]{2,1,0:T(8,128)(2,1)}, f32[13,8,512]{2,1,0:T(8,128)}) custom-call(bf16[512,1024]{1,0:T(8,128)(2,1)} %get-tuple-element.10.mo, bf16[8,512,128]{2,1,0:T(8,128)(2,1)} %get-tuple-element.11.dq, ...), custom_call_target="tpu_custom_call" | custom-call | tf_op jit(solution)/shard_map/pallas_call | solution.py:496

commit v4 on v3

--- a/solution.py
+++ b/solution.py
@@ -213,7 +213,7 @@
         loads[3].wait()
         loads[4].wait()
 
-        MB = min(256, NH * HD)
+        MB = min(512, NH * HD)
 
         def add_mix(slot, src, part, first, last):
             cols = pl.ds(pl.multiple_of(src * FS, FS), FS)

time: 83.5 us -> 80.9 us (0.969)
  Pallas kernels: 82.7 us -> 80 us
    pallas_call x1, Pallas kernels: 77.9 us -> 75.3 us  [on_device(): pl.pallas_call(kernel, out_shape=(jax.ShapeDtypeStruct((T, FS), BF16), ja...]
where the time goes in v4:
time: 80.9 us; the launch traced here: 80.7 us
  Pallas kernels  80 us (99%)
    pallas_call x1, Pallas kernels, on_device(): pl.pallas_call(kernel, out_shape=(jax.ShapeDtypeStruct((T, FS), BF16), ja...  75.3 us
    pallas_call x1, Pallas kernels, lay_out(): pl.pallas_call(lay_out_kernel, grid=(T // TILE,), out_shape=(jax.ShapeDty...  4.76 us

profile of v4, /device:TPU:0, one launch (start us, length us, event | category | flops | bytes accessed | tf_op | source)
XLA Modules:
  0.0 80.7 jit_solution(1097654321749627340)
XLA Ops:
  0.6 75.3 %shard_map.101 = (bf16[512,1024]{1,0:T(8,128)(2,1)}, bf16[8,512,128]{2,1,0:T(8,128)(2,1)}, bf16[8,512,128]{2,1,0:T(8,128)(2,1)}, bf16[8,512,128]{2,1,0:T(8,128)(2,1)}, f32[13,8,512]{2,1,0:T(8,128)}) custom-call(bf16[512,8,128]{2,1,0:T(8,128)(2,1)} %q_hbm.1, bf16[512,8,128]{2,1,0:T(8,128)(2,1)} %k_hbm.1, bf16[512,8,128]{2,1,0:T(8,128)(2,1)} %v_hbm.1, ...), custom_call_target="tpu_custom_call" | custom-call | tf_op jit(solution)/shard_map/pallas_call | solution.py:520
  75.9 4.8 %shard_map.102 = (bf16[512,1024]{1,0:T(8,128)(2,1)}, bf16[512,8,128]{2,1,0:T(8,128)(2,1)}, bf16[512,8,128]{2,1,0:T(8,128)(2,1)}, bf16[512,8,128]{2,1,0:T(8,128)(2,1)}, f32[13,8,512]{2,1,0:T(8,128)}) custom-call(bf16[512,1024]{1,0:T(8,128)(2,1)} %get-tuple-element.10.mo, bf16[8,512,128]{2,1,0:T(8,128)(2,1)} %get-tuple-element.11.dq, ...), custom_call_target="tpu_custom_call" | custom-call | tf_op jit(solution)/shard_map/pallas_call | solution.py:496
